TPU v7x, 32 devices: a whole 2x2x4 slice. The times are simulated.
32 devices in a mesh: group: 2 (over y), gx: 4 (over z), gz: 2 (over x), col: 2 (over core).
Axes of the slice: x: 2, y: 2, z: 4, core: 2. Of those that a mesh axis runs over, the one named last changes fastest.
Arguments:
- features: bfloat16 [32, 64, 16, 256], P(None, 'col', ('group', 'gx'), 'gz'), parts along dimension 2, may hold values from -6 to 6
- labels: int32 [64, 16, 256], P(None, ('group', 'gx'), 'gz'), parts along dimension 1, may hold values from 0 to 3
- grid_index: int32 [64], replicated, may hold values from 0 to 15
- stretch: float32 [16, 9], replicated, may hold values from 0.5 to 2
- tile_filter: float32 [32, 25], replicated, may hold values from -1.25 to 1.25
- wall_filter: float32 [32, 9], replicated, may hold values from -2 to 2
- class_weight: float32 [4, 32], replicated, may hold values from -1 to 1
Outputs:
- grad_features: bfloat16 [32, 64, 16, 256], P(None, 'col', ('group', 'gx'), 'gz'), parts along dimension 2
- grad_tile_filter: float32 [64, 25], P('group'), parts along dimension 0
- grad_wall_filter: float32 [64, 9], P('group'), parts along dimension 0
- grad_class_weight: float32 [8, 32], P('group'), parts along dimension 0
There are 2 independent parts, one for each index of `group`. A program takes and returns all parts, laid end to end along the dimension named above; an argument that names none is the same for every part. Nothing has to cross between parts.
All inputs are finite; a program needn't handle non-finite values.
Results may differ from a plain program's by a relative error of at most 0.0064.
Values may be sent and summed in bfloat16 or wider, within the bound.
A program may use at most 64 MiB of HBM per device.

v0:
```python
import jax
import jax.numpy as jnp
from jax import lax
from jax.sharding import PartitionSpec as P


def with_halo(value, sides, width):
    for axis, dim in sides:
        size, length = (lax.axis_size(axis), value.shape[dim])
        up = [(i, (i + 1) % size) for i in range(size)]
        down = [(j, i) for i, j in up]
        last = lax.slice_in_dim(value, length - width, length, axis=dim)
        leading = lax.slice_in_dim(value, 0, width, axis=dim)
        before = lax.ppermute(last, axis, up)
        after = lax.ppermute(leading, axis, down)
        value = jnp.concatenate([before, value, after], axis=dim)
    return value


def rim_tiles(field):
    return with_halo(field, (("gx", 2), ("gz", 3)), 2)


def band_table(grid_index, stretch):
    levels = stretch.shape[0]
    onehot = (grid_index[:, None] == jnp.arange(levels, dtype=jnp.int32)[None, :]).astype(
        jnp.float32
    )
    return jnp.dot(onehot, stretch, precision=lax.Precision.HIGHEST)


def wall_forward(smooth_ext, wall_rows, band_rows):
    rows = band_rows.shape[0]
    total = jnp.zeros((smooth_ext.shape[0], rows) + smooth_ext.shape[2:], jnp.float32)
    for k in range(9):
        tap = wall_rows[:, k][:, None] * band_rows[:, k][None, :]
        total = total + tap[:, :, None, None] * smooth_ext[:, k : k + rows].astype(jnp.float32)
    return total


def wall_backward(grad_ext, wall_rows, band_ext, rows):
    total = jnp.zeros((grad_ext.shape[0], rows) + grad_ext.shape[2:], jnp.float32)
    for k in range(9):
        first = 8 - k
        tap = wall_rows[:, k][:, None] * band_ext[first : first + rows, k][None, :]
        total = total + tap[:, :, None, None] * grad_ext[:, first : first + rows].astype(
            jnp.float32
        )
    return total


def shards(features, labels, grid_index, stretch, tile_filter, wall_filter, class_weight):
    chans, half_rows, cells_x, cells_z = features.shape
    all_rows = labels.shape[0]
    classes = class_weight.shape[0]
    volume = all_rows * cells_x * lax.axis_size("gx") * cells_z * lax.axis_size("gz")
    widened = rim_tiles(features)
    smooth = jnp.zeros(features.shape, jnp.float32)
    for i in range(5):
        for j in range(5):
            weight = tile_filter[:, 5 * i + j][:, None, None, None]
            smooth = smooth + weight * widened[:, :, i : i + cells_x, j : j + cells_z].astype(
                jnp.float32
            )
    smoothed = smooth.astype(jnp.bfloat16)
    bands = band_table(grid_index, stretch)
    bands_pad = jnp.pad(bands, ((4, 4), (0, 0)))
    place = lax.axis_index("col")
    share = chans // lax.axis_size("col")
    first_chan = place * share
    pencil = lax.all_to_all(smoothed, "col", split_axis=0, concat_axis=1, tiled=True)
    smooth_ext = jnp.pad(pencil, ((0, 0), (4, 4), (0, 0), (0, 0)))
    wall_rows = lax.dynamic_slice_in_dim(wall_filter, first_chan, share, 0)
    class_rows = lax.dynamic_slice_in_dim(class_weight, first_chan, share, 1)
    wall_out = wall_forward(smooth_ext, wall_rows, bands)
    sig = jax.nn.sigmoid(wall_out)
    hidden = wall_out * sig
    partial_scores = jnp.einsum(
        "kc,cyxz->kyxz", class_rows, hidden, precision=lax.Precision.HIGHEST
    )
    scores = lax.psum(partial_scores, "col")
    targets = (labels[None] == jnp.arange(classes, dtype=jnp.int32)[:, None, None, None]).astype(
        jnp.float32
    )
    errors = scores - targets
    grad_hidden = jnp.einsum("kc,kyxz->cyxz", class_rows, errors, precision=lax.Precision.HIGHEST)
    grad_wall = (grad_hidden * sig * (1.0 + wall_out * (1.0 - sig))).astype(jnp.bfloat16)
    class_part = jnp.einsum("kyxz,cyxz->kc", errors, hidden, precision=lax.Precision.HIGHEST)
    grad_vals = grad_wall.astype(jnp.float32)
    wall_part = jnp.stack(
        [
            jnp.sum(
                grad_vals
                * bands[:, k][None, :, None, None]
                * smooth_ext[:, k : k + all_rows].astype(jnp.float32),
                axis=(1, 2, 3),
            )
            for k in range(9)
        ],
        axis=1,
    )
    grad_ext = jnp.pad(grad_wall, ((0, 0), (4, 4), (0, 0), (0, 0)))
    grad_smooth = wall_backward(grad_ext, wall_rows, bands_pad, all_rows).astype(jnp.bfloat16)
    grad_tile = lax.all_to_all(grad_smooth, "col", split_axis=1, concat_axis=0, tiled=True)
    wall_full = lax.dynamic_update_slice_in_dim(
        jnp.zeros((chans, 9), jnp.float32), wall_part, first_chan, 0
    )
    class_full = lax.dynamic_update_slice_in_dim(
        jnp.zeros((classes, chans), jnp.float32), class_part, first_chan, 1
    )
    grad_widened = rim_tiles(grad_tile)
    grad_tile_vals = grad_tile.astype(jnp.float32)
    grad_field = jnp.zeros(features.shape, jnp.float32)
    tile_terms = []
    for i in range(5):
        for j in range(5):
            weight = tile_filter[:, 5 * i + j][:, None, None, None]
            grad_field = grad_field + weight * grad_widened[
                :, :, 4 - i : 4 - i + cells_x, 4 - j : 4 - j + cells_z
            ].astype(jnp.float32)
            shifted = widened[:, :, i : i + cells_x, j : j + cells_z].astype(jnp.float32)
            tile_terms.append(jnp.sum(shifted * grad_tile_vals, axis=(1, 2, 3)))
    tile_part = jnp.stack(tile_terms, axis=1)
    totals = lax.psum((tile_part, wall_full, class_full), ("gx", "gz", "col"))
    return (
        grad_field.astype(jnp.bfloat16),
        totals[0] / volume,
        totals[1] / volume,
        totals[2] / volume,
    )


def solution(mesh):
    return jax.shard_map(
        shards,
        mesh=mesh,
        in_specs=(
            P(None, "col", ("group", "gx"), "gz"),
            P(None, ("group", "gx"), "gz"),
            P(),
            P(),
            P(),
            P(),
            P(),
        ),
        out_specs=(
            P(None, "col", ("group", "gx"), "gz"),
            P("group", None),
            P("group", None),
            P("group", None),
        ),
        check_vma=False,
    )
```

profile of v0, /device:TPU:0, one launch (start us, length us, event | category | flops | bytes accessed | tf_op | source)
XLA Modules:
  0.0 227.5 jit_solution(17064217156550470900)
XLA Ops:
  7.2 0.0 copy-start
  7.2 0.0 all-reduce.6.cloned.1.call-start
  7.2 1.1 copy.53
  8.4 3.1 %collective-permute-start = (bf16[32,32,2,128]{3,1,2,0:T(8,128)(2,1)S(1)}, bf16[32,32,2,128]{3,1,2,0:T(8,128)(2,1)S(1)}, u32[]{:S(2)}, u32[]{:S(2)}) collective-permute-start(bf16[32,32,2,128]{3,1,2,0:T(8,128)(2,1)S(1)} %copy.53), channel_id=1, source_target_pairs={{0,4},{4,8},{8,12},{12,0},{1,5},{5,9},{9,13},{13,1},{2,6},{6,10},{... | collective-permute-start | bytes 1572872 | tf_op jit(solution)/shard_map/ppermute | solution.py:14
  11.5 2.1 collective-permute-start.1
  13.6 0.8 fusion.110
  14.4 0.1 fusion.117
  14.6 1.1 dynamic-slice_bitcast_fusion.8
  15.7 0.7 broadcast_multiply_fusion.4
  16.4 0.7 broadcast_multiply_fusion.2
  17.1 0.7 broadcast_multiply_fusion
  17.8 0.1 broadcast_multiply_fusion.6
  18.0 0.1 broadcast_multiply_fusion.16
  18.1 2.5 %slice_reduce_fusion.24 = (f32[32]{0:T(128)S(1)}, f32[32]{0:T(128)S(1)}, f32[32]{0:T(128)S(1)}, f32[32]{0:T(128)S(1)}, f32[32]{0:T(128)S(1)}, /*index=5*/f32[32]...) fusion(f32[32,25]{1,0:T(8,128)} %param.11), kind=kLoop, calls=%fused_computation.296 | loop fusion | bytes 4864 | tf_op jit(solution)/shard_map/slice | solution.py:117
  20.6 5.7 %collective-permute-done = bf16[32,32,2,128]{3,1,2,0:T(8,128)(2,1)S(1)} collective-permute-done((bf16[32,32,2,128]{3,1,2,0:T(8,128)(2,1)S(1)}, bf16[32,32,2,128]{3,1,2,0:T(8,128)(2,1)S(1)}, u32[]{:S(2)}, u32[]{:S(2)}) %collective-permute-start) | collective-permute-done | bytes 524320 | tf_op jit(solution)/shard_map/ppermute | solution.py:14
  26.3 1.4 constant_dynamic-update-slice_fusion.1
  27.7 8.4 %collective-permute-done.1 = bf16[32,32,2,128]{3,1,2,0:T(8,128)(2,1)S(1)} collective-permute-done((bf16[32,32,2,128]{3,1,2,0:T(8,128)(2,1)S(1)}, bf16[32,32,2,128]{3,1,2,0:T(8,128)(2,1)S(1)}, u32[]{:S(2)}, u32[]{:S(2)}) %collective-permute-start.1) | collective-permute-done | bytes 524320 | tf_op jit(solution)/shard_map/ppermute | solution.py:15
  36.1 0.8 copy-done.9
  36.9 0.1 constant_dynamic-update-slice_fusion
  37.0 1.9 fusion.129
  38.9 3.1 %copy.56 = bf16[32,32,6,2]{1,0,3,2:T(8,128)(2,1)} copy(bf16[32,32,6,2]{3,1,2,0:T(8,128)(2,1)} %get-tuple-element.96) | data formatting | bytes 49152 | tf_op jit(solution)/shard_map/slice | solution.py:12
  42.0 1.5 collective-permute-start.2
  43.5 2.1 copy.58
  45.6 0.5 collective-permute-start.3
  46.2 0.8 slice_reduce_fusion.23
  47.0 2.2 copy.57
  49.2 1.4 collective-permute-done.3
  50.6 3.0 %copy.59 = bf16[32,32,6,2]{3,1,2,0:T(8,128)(2,1)} copy(bf16[32,32,6,2]{1,0,3,2:T(8,128)(2,1)} %collective-permute-done.3) | data formatting | bytes 49152 | tf_op jit(solution)/shard_map/ppermute | solution.py:15
  53.5 11.2 %fusion.90 = (bf16[32,32,2,128]{3,1,2,0:T(8,128)(2,1)S(1)}, bf16[32,32,2,128]{3,1,2,0:T(8,128)(2,1)}, bf16[32,32,2,128]{3,1,2,0:T(8,128)(2,1)}) fusion(bf16[32,32,2,128]{3,1,2,0:T(8,128)(2,1)} %copy-done.9, bf16[32,32,2,128]{3,1,2,0:T(8,128)(2,1)} %copy-done.5, bf16[32,32,2,128]{3,1,2,0:T(8,128)(2,1)} %copy-done.7, f32[32]{0:T(128)} %get-tuple-element.81, ...), kind=kLoop, calls=%fused_computation.211 | loop fusion | flops 37486592 | bytes 4770944 | tf_op jit(solution)/shard_map/convert_element_type | solution.py:65
  64.8 4.2 %all_to_all.36 = bf16[32,32,2,128]{3,1,2,0:T(8,128)(2,1)S(1)} all-to-all(bf16[32,32,2,128]{3,1,2,0:T(8,128)(2,1)S(1)} %get-tuple-element.88), channel_id=1, replica_groups=mesh['group'=2,'gx'=4,'gz'=2,'col'=2] {'col'}, dimensions={0} | all-to-all | bytes 1048576 | tf_op jit(solution)/shard_map/all_to_all | solution.py:71
  68.9 0.3 copy.63
  69.2 2.7 %fusion.88 = (f32[16,64,2,128]{3,0,2,1:T(8,128)S(1)}, f32[16,64,2,128]{3,0,2,1:T(8,128)}) fusion(f32[16,64]{0,1:T(8,128)S(1)} %get-tuple-element.138, f32[16,64]{0,1:T(8,128)S(1)} %get-tuple-element.140, f32[16,64]{0,1:T(8,128)S(1)} %get-tuple-element.134, f32[16,64]{0,1:T(8,128)S(1)} %get-tuple-element.142, bf16[16,64,2,128]{3,0,2,1:T(8,128)(2,1)S(1)} %bitcast.143, ...), kind=kLoop, calls=%fused_computation.209 | loop fusion | flops 7864320 | bytes 2658304 | tf_op jit(solution)/shard_map/mul | solution.py:77
  72.0 1.3 fusion.113
  73.3 0.0 all-reduce.6.cloned.1.call-update
  73.4 18.9 %all-reduce.6.cloned.1.call-done = f32[4,64,2,128]{3,0,2,1:T(4,128)} async-done(((f32[4,64,2,128]{3,0,2,1:T(4,128)}), f32[4,64,2,128]{3,0,2,1:T(4,128)}) %all-reduce.6.cloned.1.call-update) | async-done | bytes 262160 | tf_op jit(solution)/shard_map/psum | solution.py:81
  92.3 4.8 %fusion.42 = (f32[16]{0:T(128)S(1)}, f32[16]{0:T(128)S(1)}, f32[16]{0:T(128)S(1)}, f32[16]{0:T(128)S(1)}, f32[16]{0:T(128)S(1)}, /*index=5*/f32[16]{0:T(128)S(1)...) fusion(f32[64]{0:T(128)} %copy-done.40, ...), kind=kOutput, calls=%fused_computation.162 | convolution fusion | flops 24838000 | bytes 2952516 | tf_op jit(solution)/shard_map/kc,kyxz->cyxz/dot_general | solution.py:86
  97.2 1.7 fusion.48
  99.0 4.3 %all_to_all.37 = bf16[16,64,2,128]{3,0,2,1:T(8,128)(2,1)S(1)} all-to-all(bf16[16,64,2,128]{3,0,2,1:T(8,128)(2,1)S(1)} %fusion.48), channel_id=1, replica_groups=mesh['group'=2,'gx'=4,'gz'=2,'col'=2] {'col'}, dimensions={1} | all-to-all | bytes 1048576 | tf_op jit(solution)/shard_map/all_to_all | solution.py:104
  103.2 0.2 copy.64
  103.5 3.9 %fusion.85 = (f32[32]{0:T(128)S(1)}, f32[32]{0:T(128)S(1)}, f32[32]{0:T(128)S(1)}, f32[32]{0:T(128)S(1)}, f32[32]{0:T(128)S(1)}, /*index=5*/f32[32]{0:T(128)S(1)}, f32[32]{0:T(128)S(1)}, f32[32]{0:T(128)S(1)}, f32[32]{0:T(128)S(1)}) fusion(bf16[2,16,32,2,128]{4,2,3,1,0:T(8,128)(2,1)S(1)} %copy.64, bf16[32,32,6,2]{3,1,2,0:T(8,128)(2,1)S(1)} %copy-done.3, ...), kind=kLoop, calls=%fused_computation.205 | loop fusion | flops 14417632 | bytes 2122880 | tf_op jit(solution)/shard_map/reduce_sum | solution.py:122
  107.5 3.8 %fusion.82 = (f32[32]{0:T(128)S(1)}, f32[32]{0:T(128)S(1)}, f32[32]{0:T(128)S(1)}, f32[32]{0:T(128)S(1)}, f32[32]{0:T(128)S(1)}, /*index=5*/f32[32]{0:T(128)S(1)}, f32[32]{0:T(128)S(1)}, f32[32]{0:T(128)S(1)}, f32[32]{0:T(128)S(1)}) fusion(bf16[2,16,32,2,128]{4,2,3,1,0:T(8,128)(2,1)S(1)} %copy.64, ...), kind=kLoop, calls=%fused_computation.202 | loop fusion | flops 14417632 | bytes 2122880 | tf_op jit(solution)/shard_map/reduce_sum | solution.py:122
  111.2 1.8 collective-permute-start.4
  113.0 2.1 collective-permute-start.5
  115.1 1.1 fusion.84
  116.2 1.4 convolution_bitcast_fusion
  117.7 0.2 dynamic_update_slice.6
  117.9 0.1 dynamic_update_slice.7
  118.1 0.1 stack.133
  118.2 72.8 %all-reduce.3 = (f32[32,25]{0,1:T(8,128)S(1)}, f32[32,9]{0,1:T(8,128)S(1)}, f32[4,32]{1,0:T(4,128)S(1)}) all-reduce(f32[32,25]{0,1:T(8,128)S(1)} %stack.133, f32[32,9]{0,1:T(8,128)S(1)} %dynamic_update_slice.6, f32[4,32]{1,0:T(4,128)S(1)} %dynamic_update_slice.7), channel_id=1, replica_groups=mesh['group'=2,'gx'=4,'gz'=2,'col'=2] {'gx','gz','col'}, use_global_device_ids=true, to_apply=%region_26.27 | all-reduce | flops 1216 | bytes 9728 | tf_op jit(solution)/shard_map/psum | solution.py:124
  191.0 0.6 broadcast_multiply_fusion.18
  191.6 0.8 copy-done.12
  192.4 1.4 pad_maximum_fusion.1
  193.7 2.4 %fusion.128 = (bf16[32,32,6,2]{3,1,2,0:T(8,128)(2,1)}, bf16[32,32,6,2]{3,1,2,0:T(8,128)(2,1)}) fusion(bf16[32,32,6,128]{3,1,2,0:T(8,128)(2,1)S(1)} %pad_maximum_fusion.1), kind=kLoop, calls=%fused_computation.344 | loop fusion | bytes 98304 | tf_op jit(solution)/shard_map/slice | solution.py:13
  196.2 2.6 %copy.75 = bf16[32,32,6,2]{1,0,3,2:T(8,128)(2,1)S(1)} copy(bf16[32,32,6,2]{3,1,2,0:T(8,128)(2,1)} %get-tuple-element.93) | data formatting | bytes 49152
  198.8 0.1 collective-permute-start.6
  198.8 2.5 %copy.76 = bf16[32,32,6,2]{1,0,3,2:T(8,128)(2,1)S(1)} copy(bf16[32,32,6,2]{3,1,2,0:T(8,128)(2,1)} %get-tuple-element.94) | data formatting | bytes 49152
  201.4 2.1 collective-permute-start.7
  203.4 0.6 broadcast_multiply_fusion.19
  204.0 0.7 copy.72
  204.7 1.4 copy.66
  206.1 2.2 copy.68
  208.5 4.3 %pad_maximum_fusion = (bf16[32,32,6,130]{3,1,2,0:T(8,128)(2,1)S(1)}, bf16[32,32,6,130]{3,1,2,0:T(8,128)(2,1)S(1)}) fusion(bf16[32,32,6,2]{3,1,2,0:T(8,128)(2,1)S(1)} %copy.66, bf16[32,32,2,128]{3,1,2,0:T(8,128)(2,1)} %collective-permute-done.5, bf16[32,32,2,128]{3,1,2,0:T(8,128)(2,1)S(1)} %bitcast.139, bf16[32,32,2,128]{3,1,2,0:T(8,128)(2,1)S(1)} %copy-done.13, ...), kind=kLoop, calls=%fused_computation.72 | loop fusion | flops 12779520 | bytes 4816896 | tf_op jit(solution)/shard_map/concatenate | solution.py:16
  212.9 6.4 %fusion.89 = bf16[32,32,2,128]{3,1,2,0:T(8,128)(2,1)S(1)} fusion(bf16[32,32,2,128]{3,1,2,0:T(8,128)(2,1)S(1)} %copy-done.13, bf16[32,32,2,128]{3,1,2,0:T(8,128)(2,1)S(1)} %bitcast.140, bf16[32,32,2,128]{3,1,2,0:T(8,128)(2,1)} %collective-permute-done.5, bf16[32,32,6,130]{3,1,2,0:T(8,128)(2,1)S(1)} %get-tuple-element.92, ...), kind=kLoop, calls=%fused_computation.210 | loop fusion | flops 20185088 | bytes 12586112 | tf_op jit(solution)/shard_map/convert_element_type | solution.py:126
  219.3 1.3 copy.71
  (105 shorter events, 0.3 us)
Async XLA Ops:
  7.2 6.4 %copy-start = (f32[16,9]{1,0:T(8,128)S(1)}, f32[16,9]{1,0:T(8,128)}, u32[]{:S(2)}) copy-start(f32[16,9]{1,0:T(8,128)} %param.10) | copy-start | bytes 1732
  7.2 85.1 %all-reduce.6.cloned.1.call-start = ((), (), s32[]{:S(2)}) async-start(), calls=%async_computation.2 | async-start | bytes 524288 | tf_op jit(solution)/shard_map/psum | solution.py:81
  8.4 27.7 %copy-start.5 = (bf16[32,32,2,128]{3,1,2,0:T(8,128)(2,1)}, bf16[32,32,2,128]{3,1,2,0:T(8,128)(2,1)S(1)}, u32[]{:S(2)}) copy-start(bf16[32,32,2,128]{3,1,2,0:T(8,128)(2,1)S(1)} %copy.53) | copy-start | bytes 1572868
  8.4 17.9 %collective-permute-start = (bf16[32,32,2,128]{3,1,2,0:T(8,128)(2,1)S(1)}, bf16[32,32,2,128]{3,1,2,0:T(8,128)(2,1)S(1)}, u32[]{:S(2)}, u32[]{:S(2)}) collective-permute-start(bf16[32,32,2,128]{3,1,2,0:T(8,128)(2,1)S(1)} %copy.53), channel_id=1, source_target_pairs={{0,4},{4,8},{8,12},{12,0},{1,5},{5,9},{9,13},{13,1},{2,6},{6,10},{... | collective-permute-start | bytes 1572872 | tf_op jit(solution)/shard_map/ppermute | solution.py:14
  11.5 24.6 %collective-permute-start.1 = (bf16[32,32,2,128]{3,1,2,0:T(8,128)(2,1)S(1)}, bf16[32,32,2,128]{3,1,2,0:T(8,128)(2,1)S(1)}, u32[]{:S(2)}, u32[]{:S(2)}) collective-permute-start(bf16[32,32,2,128]{3,1,2,0:T(8,128)(2,1)S(1)} %copy.53), channel_id=1, source_target_pairs={{4,0},{8,4},{12,8},{0,12},{5,1},{9,5},{13,9},{1,13},{6,2},{10,6},{... | collective-permute-start | bytes 1572872 | tf_op jit(solution)/shard_map/ppermute | solution.py:15
  14.5 3.3 %copy-start.40 = (f32[64]{0:T(128)}, f32[64]{0:T(128)S(1)}, u32[]{:S(2)}) copy-start(f32[64]{0:T(128)S(1)} %get-tuple-element.105) | copy-start | bytes 772
  14.5 3.3 %copy-start.41 = (f32[64]{0:T(128)}, f32[64]{0:T(128)S(1)}, u32[]{:S(2)}) copy-start(f32[64]{0:T(128)S(1)} %get-tuple-element.106) | copy-start | bytes 772
  14.5 3.3 %copy-start.42 = (f32[64]{0:T(128)}, f32[64]{0:T(128)S(1)}, u32[]{:S(2)}) copy-start(f32[64]{0:T(128)S(1)} %get-tuple-element.107) | copy-start | bytes 772
  14.5 3.3 %copy-start.43 = (f32[64]{0:T(128)}, f32[64]{0:T(128)S(1)}, u32[]{:S(2)}) copy-start(f32[64]{0:T(128)S(1)} %get-tuple-element.108) | copy-start | bytes 772
  14.6 3.3 %copy-start.45 = (f32[64]{0:T(128)}, f32[64]{0:T(128)S(1)}, u32[]{:S(2)}) copy-start(f32[64]{0:T(128)S(1)} %get-tuple-element.110) | copy-start | bytes 772
  14.6 3.3 %copy-start.46 = (f32[64]{0:T(128)}, f32[64]{0:T(128)S(1)}, u32[]{:S(2)}) copy-start(f32[64]{0:T(128)S(1)} %get-tuple-element.111) | copy-start | bytes 772
  14.6 3.4 %copy-start.44 = (f32[64]{0:T(128)}, f32[64]{0:T(128)S(1)}, u32[]{:S(2)}) copy-start(f32[64]{0:T(128)S(1)} %get-tuple-element.109) | copy-start | bytes 772
  14.6 3.4 %copy-start.47 = (f32[64]{0:T(128)}, f32[64]{0:T(128)S(1)}, u32[]{:S(2)}) copy-start(f32[64]{0:T(128)S(1)} %get-tuple-element.112) | copy-start | bytes 772
  14.6 6.0 %copy-start.48 = (f32[64]{0:T(128)}, f32[64]{0:T(128)S(1)}, u32[]{:S(2)}) copy-start(f32[64]{0:T(128)S(1)} %get-tuple-element.113) | copy-start | bytes 772
  26.3 9.8 %copy-start.7 = (bf16[32,32,2,128]{3,1,2,0:T(8,128)(2,1)}, bf16[32,32,2,128]{3,1,2,0:T(8,128)(2,1)S(1)}, u32[]{:S(2)}) copy-start(bf16[32,32,2,128]{3,1,2,0:T(8,128)(2,1)S(1)} %collective-permute-done) | copy-start | bytes 1572868
  36.1 0.8 copy-start.9
  38.9 7.3 %copy-start.4 = (f32[32,25]{1,0:T(8,128)S(1)}, f32[32,25]{1,0:T(8,128)}, u32[]{:S(2)}) copy-start(f32[32,25]{1,0:T(8,128)} %param.11) | copy-start | bytes 9604
  42.0 5.0 %collective-permute-start.2 = (bf16[32,32,6,2]{1,0,3,2:T(8,128)(2,1)}, bf16[32,32,6,2]{1,0,3,2:T(8,128)(2,1)}, u32[]{:S(2)}, u32[]{:S(2)}) collective-permute-start(bf16[32,32,6,2]{1,0,3,2:T(8,128)(2,1)} %copy.56), channel_id=1, source_target_pairs={{0,2},{2,0},{1,3},{3,1},{4,6},{6,4},{5,7},{7,5},{8,10},{10,8},{9,1... | collective-permute-start | bytes 73736 | tf_op jit(solution)/shard_map/ppermute | solution.py:14
  45.6 4.9 %collective-permute-start.3 = (bf16[32,32,6,2]{1,0,3,2:T(8,128)(2,1)}, bf16[32,32,6,2]{1,0,3,2:T(8,128)(2,1)}, u32[]{:S(2)}, u32[]{:S(2)}) collective-permute-start(bf16[32,32,6,2]{1,0,3,2:T(8,128)(2,1)} %copy.58), channel_id=1, source_target_pairs={{2,0},{0,2},{3,1},{1,3},{6,4},{4,6},{7,5},{5,7},{10,8},{8,10},{11,... | collective-permute-start | bytes 73736 | tf_op jit(solution)/shard_map/ppermute | solution.py:15
  49.2 15.6 %copy-start.1 = (bf16[32,32,6,2]{3,1,2,0:T(8,128)(2,1)}, bf16[32,32,6,2]{3,1,2,0:T(8,128)(2,1)S(1)}, u32[]{:S(2)}) copy-start(bf16[32,32,6,2]{3,1,2,0:T(8,128)(2,1)S(1)} %copy.57) | copy-start | bytes 73732
  64.7 7.2 %copy-start.39 = (f32[4,32]{1,0:T(4,128)S(1)}, f32[4,32]{1,0:T(4,128)}, u32[]{:S(2)}) copy-start(f32[4,32]{1,0:T(4,128)} %param.13) | copy-start | bytes 1540
  92.3 4.9 %copy-start.17 = (f32[16,64]{0,1:T(8,128)S(1)}, f32[16,64]{0,1:T(8,128)}, u32[]{:S(2)}) copy-start(f32[16,64]{0,1:T(8,128)} %get-tuple-element.129) | copy-start | bytes 12292
  92.3 4.9 %copy-start.18 = (f32[16,64]{0,1:T(8,128)S(1)}, f32[16,64]{0,1:T(8,128)}, u32[]{:S(2)}) copy-start(f32[16,64]{0,1:T(8,128)} %get-tuple-element.145) | copy-start | bytes 12292
  92.3 4.9 %copy-start.19 = (f32[16,64]{0,1:T(8,128)S(1)}, f32[16,64]{0,1:T(8,128)}, u32[]{:S(2)}) copy-start(f32[16,64]{0,1:T(8,128)} %get-tuple-element.133) | copy-start | bytes 12292
  92.3 4.9 %copy-start.20 = (f32[16,64]{0,1:T(8,128)S(1)}, f32[16,64]{0,1:T(8,128)}, u32[]{:S(2)}) copy-start(f32[16,64]{0,1:T(8,128)} %get-tuple-element.143) | copy-start | bytes 12292
  92.3 4.9 %copy-start.21 = (f32[16,64]{0,1:T(8,128)S(1)}, f32[16,64]{0,1:T(8,128)}, u32[]{:S(2)}) copy-start(f32[16,64]{0,1:T(8,128)} %get-tuple-element.137) | copy-start | bytes 12292
  92.3 4.9 %copy-start.22 = (f32[16,64]{0,1:T(8,128)S(1)}, f32[16,64]{0,1:T(8,128)}, u32[]{:S(2)}) copy-start(f32[16,64]{0,1:T(8,128)} %get-tuple-element.141) | copy-start | bytes 12292
  97.1 6.3 %copy-start.3 = (bf16[32,32,6,2]{3,1,2,0:T(8,128)(2,1)S(1)}, bf16[32,32,6,2]{3,1,2,0:T(8,128)(2,1)}, u32[]{:S(2)}) copy-start(bf16[32,32,6,2]{3,1,2,0:T(8,128)(2,1)} %copy.59) | copy-start | bytes 73732
  98.9 8.5 %copy-start.2 = (bf16[32,32,6,2]{3,1,2,0:T(8,128)(2,1)S(1)}, bf16[32,32,6,2]{3,1,2,0:T(8,128)(2,1)}, u32[]{:S(2)}) copy-start(bf16[32,32,6,2]{3,1,2,0:T(8,128)(2,1)} %copy-done.1) | copy-start | bytes 73732
  103.5 11.6 %copy-start.6 = (bf16[32,32,2,128]{3,1,2,0:T(8,128)(2,1)S(1)}, bf16[32,32,2,128]{3,1,2,0:T(8,128)(2,1)}, u32[]{:S(2)}) copy-start(bf16[32,32,2,128]{3,1,2,0:T(8,128)(2,1)} %copy-done.5) | copy-start | bytes 1572868
  103.5 11.6 %copy-start.8 = (bf16[32,32,2,128]{3,1,2,0:T(8,128)(2,1)S(1)}, bf16[32,32,2,128]{3,1,2,0:T(8,128)(2,1)}, u32[]{:S(2)}) copy-start(bf16[32,32,2,128]{3,1,2,0:T(8,128)(2,1)} %copy-done.7) | copy-start | bytes 1572868
  103.5 11.6 %copy-start.10 = (bf16[32,32,2,128]{3,1,2,0:T(8,128)(2,1)S(1)}, bf16[32,32,2,128]{3,1,2,0:T(8,128)(2,1)}, u32[]{:S(2)}) copy-start(bf16[32,32,2,128]{3,1,2,0:T(8,128)(2,1)} %copy-done.9) | copy-start | bytes 1572868
  103.5 11.6 %copy-start.11 = (bf16[32,32,2,128]{3,2,1,0:T(2,128)(2,1)S(1)}, bf16[32,32,2,128]{3,2,1,0:T(2,128)(2,1)}, u32[]{:S(2)}) copy-start(bf16[32,32,2,128]{3,2,1,0:T(2,128)(2,1)} %param.7) | copy-start | bytes 1572868
  103.5 11.6 %copy-start.14 = (bf16[32,32,2,128]{3,1,2,0:T(8,128)(2,1)S(1)}, bf16[32,32,2,128]{3,1,2,0:T(8,128)(2,1)}, u32[]{:S(2)}) copy-start(bf16[32,32,2,128]{3,1,2,0:T(8,128)(2,1)} %get-tuple-element.89) | copy-start | bytes 1572868
  103.5 11.6 %copy-start.15 = (bf16[32,32,2,128]{3,1,2,0:T(8,128)(2,1)S(1)}, bf16[32,32,2,128]{3,1,2,0:T(8,128)(2,1)}, u32[]{:S(2)}) copy-start(bf16[32,32,2,128]{3,1,2,0:T(8,128)(2,1)} %get-tuple-element.90) | copy-start | bytes 1572868
  107.4 8.8 %copy-start.16 = (f32[4,64,2,128]{3,0,2,1:T(4,128)S(1)}, f32[4,64,2,128]{3,0,2,1:T(4,128)}, u32[]{:S(2)}) copy-start(f32[4,64,2,128]{3,0,2,1:T(4,128)} %all-reduce.6.cloned.1.call-done) | copy-start | bytes 786436
  107.4 8.8 %copy-start.23 = (s32[64,2,128]{2,1,0:T(2,128)S(1)}, s32[64,2,128]{2,1,0:T(2,128)}, u32[]{:S(2)}) copy-start(s32[64,2,128]{2,1,0:T(2,128)} %param.8) | copy-start | bytes 196612
  111.2 80.3 %collective-permute-start.4 = (bf16[32,32,2,128]{3,1,2,0:T(8,128)(2,1)S(1)}, bf16[32,32,2,128]{3,1,2,0:T(8,128)(2,1)S(1)}, u32[]{:S(2)}, u32[]{:S(2)}) collective-permute-start(bf16[32,32,2,128]{3,1,2,0:T(8,128)(2,1)S(1)} %bitcast.136), channel_id=1, source_target_pairs={{0,4},{4,8},{8,12},{12,0},{1,5},{5,9},{9,13},{13,1},{2,6},{6,10},{... | collective-permute-start | bytes 1572872 | tf_op jit(solution)/shard_map/ppermute | solution.py:14
  113.0 79.4 %collective-permute-start.5 = (bf16[32,32,2,128]{3,1,2,0:T(8,128)(2,1)S(1)}, bf16[32,32,2,128]{3,1,2,0:T(8,128)(2,1)}, u32[]{:S(2)}, u32[]{:S(2)}) collective-permute-start(bf16[32,32,2,128]{3,1,2,0:T(8,128)(2,1)S(1)} %bitcast.137), channel_id=1, source_target_pairs={{4,0},{8,4},{12,8},{0,12},{5,1},{9,5},{13,9},{1,13},{6,2},{10,6},{... | collective-permute-start | bytes 1572872 | tf_op jit(solution)/shard_map/ppermute | solution.py:15
  191.6 0.8 copy-start.12
  196.2 12.2 %copy-start.13 = (bf16[32,32,2,128]{3,1,2,0:T(8,128)(2,1)S(1)}, bf16[32,32,2,128]{3,1,2,0:T(8,128)(2,1)}, u32[]{:S(2)}) copy-start(bf16[32,32,2,128]{3,1,2,0:T(8,128)(2,1)} %copy-done.12) | copy-start | bytes 1572868
  198.8 6.0 %collective-permute-start.6 = (bf16[32,32,6,2]{1,0,3,2:T(8,128)(2,1)S(1)}, bf16[32,32,6,2]{1,0,3,2:T(8,128)(2,1)S(1)}, u32[]{:S(2)}, u32[]{:S(2)}) collective-permute-start(bf16[32,32,6,2]{1,0,3,2:T(8,128)(2,1)S(1)} %copy.75), channel_id=1, source_target_pairs={{2,0},{0,2},{3,1},{1,3},{6,4},{4,6},{7,5},{5,7},{10,8},{8,10},{11,... | collective-permute-start | bytes 73736 | tf_op jit(solution)/shard_map/ppermute | solution.py:15
  201.4 4.7 %collective-permute-start.7 = (bf16[32,32,6,2]{1,0,3,2:T(8,128)(2,1)S(1)}, bf16[32,32,6,2]{1,0,3,2:T(8,128)(2,1)S(1)}, u32[]{:S(2)}, u32[]{:S(2)}) collective-permute-start(bf16[32,32,6,2]{1,0,3,2:T(8,128)(2,1)S(1)} %copy.76), channel_id=1, source_target_pairs={{0,2},{2,0},{1,3},{3,1},{4,6},{6,4},{5,7},{7,5},{8,10},{10,8},{9,1... | collective-permute-start | bytes 73736 | tf_op jit(solution)/shard_map/ppermute | solution.py:14
  208.3 4.4 %copy-start.24 = (f32[32]{0:T(128)S(1)}, f32[32]{0:T(128)}, u32[]{:S(2)}) copy-start(f32[32]{0:T(128)} %get-tuple-element.64) | copy-start | bytes 388
  208.3 4.4 %copy-start.25 = (f32[32]{0:T(128)S(1)}, f32[32]{0:T(128)}, u32[]{:S(2)}) copy-start(f32[32]{0:T(128)} %get-tuple-element.65) | copy-start | bytes 388
  208.3 4.4 %copy-start.26 = (f32[32]{0:T(128)S(1)}, f32[32]{0:T(128)}, u32[]{:S(2)}) copy-start(f32[32]{0:T(128)} %get-tuple-element.66) | copy-start | bytes 388
  208.3 4.4 %copy-start.27 = (f32[32]{0:T(128)S(1)}, f32[32]{0:T(128)}, u32[]{:S(2)}) copy-start(f32[32]{0:T(128)} %get-tuple-element.67) | copy-start | bytes 388
  208.4 4.4 %copy-start.28 = (f32[32]{0:T(128)S(1)}, f32[32]{0:T(128)}, u32[]{:S(2)}) copy-start(f32[32]{0:T(128)} %get-tuple-element.68) | copy-start | bytes 388
  208.4 4.4 %copy-start.29 = (f32[32]{0:T(128)S(1)}, f32[32]{0:T(128)}, u32[]{:S(2)}) copy-start(f32[32]{0:T(128)} %get-tuple-element.69) | copy-start | bytes 388
  208.4 4.4 %copy-start.30 = (f32[32]{0:T(128)S(1)}, f32[32]{0:T(128)}, u32[]{:S(2)}) copy-start(f32[32]{0:T(128)} %get-tuple-element.70) | copy-start | bytes 388
  208.4 4.4 %copy-start.31 = (f32[32]{0:T(128)S(1)}, f32[32]{0:T(128)}, u32[]{:S(2)}) copy-start(f32[32]{0:T(128)} %get-tuple-element.71) | copy-start | bytes 388
  208.4 4.4 %copy-start.32 = (f32[32]{0:T(128)S(1)}, f32[32]{0:T(128)}, u32[]{:S(2)}) copy-start(f32[32]{0:T(128)} %get-tuple-element.72) | copy-start | bytes 388
  208.4 4.4 %copy-start.33 = (f32[32]{0:T(128)S(1)}, f32[32]{0:T(128)}, u32[]{:S(2)}) copy-start(f32[32]{0:T(128)} %get-tuple-element.73) | copy-start | bytes 388
  208.4 4.4 %copy-start.34 = (f32[32]{0:T(128)S(1)}, f32[32]{0:T(128)}, u32[]{:S(2)}) copy-start(f32[32]{0:T(128)} %get-tuple-element.74) | copy-start | bytes 388
  208.4 4.4 %copy-start.35 = (f32[32]{0:T(128)S(1)}, f32[32]{0:T(128)}, u32[]{:S(2)}) copy-start(f32[32]{0:T(128)} %get-tuple-element.75) | copy-start | bytes 388
  208.4 4.4 %copy-start.36 = (f32[32]{0:T(128)S(1)}, f32[32]{0:T(128)}, u32[]{:S(2)}) copy-start(f32[32]{0:T(128)} %get-tuple-element.76) | copy-start | bytes 388
  208.4 4.4 %copy-start.37 = (f32[32]{0:T(128)S(1)}, f32[32]{0:T(128)}, u32[]{:S(2)}) copy-start(f32[32]{0:T(128)} %get-tuple-element.81) | copy-start | bytes 388
  208.5 4.4 %copy-start.38 = (f32[32]{0:T(128)S(1)}, f32[32]{0:T(128)}, u32[]{:S(2)}) copy-start(f32[32]{0:T(128)} %get-tuple-element.82) | copy-start | bytes 388
Sparse Core Ops, SparseCore 0:
  73.5 18.7 all-reduce.5
where the time goes:
time: 228 us; the launch traced here: 227 us
  blocking collectives  81.2 us (36%)
  other arithmetic  39.9 us (18%)
  local copies, waits for them, and re-layouts  35.5 us (16%)
  waiting for transfers between devices  34.4 us (15%)
  between operations  14.8 us (6%)
  starting transfers between devices  13.2 us (6%)
  matrix products  8.43 us (4%)
    psum x1, blocking collectives, shards(): totals = lax.psum((tile_part, wall_full, class_full), ('gx', 'gz', 'col'))  72.8 us
    psum x1, waiting for transfers between devices, shards(): scores = lax.psum(partial_scores, 'col')  18.9 us
    unnamed x105, local copies, waits for them, and re-layouts  11.5 us
    convert_element_type x1, other arithmetic, shards(): smoothed = smooth.astype(jnp.bfloat16)  11.2 us
    ppermute x4, waiting for transfers between devices, with_halo(): after = lax.ppermute(leading, axis, down)  9.77 us
    reduce_sum x3, other arithmetic, shards(): tile_terms.append(jnp.sum(shifted * grad_tile_vals, axis=(1, 2, 3)))  8.73 us
    ppermute x4, starting transfers between devices, with_halo(): before = lax.ppermute(last, axis, up)  8.43 us
    slice x3, local copies, waits for them, and re-layouts, with_halo(): leading = lax.slice_in_dim(value, 0, width, axis=dim)  6.44 us
  transfers between devices with their start and end apart: 9, of which 4 were waited for; matrix products, arithmetic and copies ran while one was open for 10% of the time, Pallas kernels for 0%

commit v1 on v0

--- a/solution.py
+++ b/solution.py
@@ -121,7 +121,7 @@
             shifted = widened[:, :, i : i + cells_x, j : j + cells_z].astype(jnp.float32)
             tile_terms.append(jnp.sum(shifted * grad_tile_vals, axis=(1, 2, 3)))
     tile_part = jnp.stack(tile_terms, axis=1)
-    totals = lax.psum((tile_part, wall_full, class_full), ("gx", "gz", "col"))
+    totals = lax.psum(lax.psum((tile_part, wall_full, class_full), ("gz", "col")), "gx")
     return (
         grad_field.astype(jnp.bfloat16),
         totals[0] / volume,

time: 228 us -> 188 us (0.82)
  blocking collectives: 81.2 us -> 39.6 us
    psum x1 -> x2, blocking collectives: 72.8 us -> 31.2 us  [the longest x1 19.1 us: shards(): lax.psum(lax.psum((tile_part, wall_full, class_full), ('gz', 'col')), 'gx')]
  transfers between devices with their start and end apart: 9 -> 9, of which waited for: 4 -> 5; matrix products, arithmetic and copies ran while one was open for 10% -> 12% of each run, Pallas kernels for 0% -> 0%
where the time goes in v1:
time: 188 us; the launch traced here: 187 us
  other arithmetic  39.9 us (21%)
  blocking collectives  39.6 us (21%)
  waiting for transfers between devices  35.7 us (19%)
  local copies, waits for them, and re-layouts  35.5 us (19%)
  between operations  14.7 us (8%)
  starting transfers between devices  13.3 us (7%)
  matrix products  8.43 us (4%)
    psum x1, blocking collectives, shards(): lax.psum(lax.psum((tile_part, wall_full, class_full), ('gz', 'col')), 'gx')  19.1 us
    psum x1, waiting for transfers between devices, shards(): scores = lax.psum(partial_scores, 'col')  18.9 us
    psum x1, blocking collectives, shards(): lax.psum((tile_part, wall_full, class_full), ('gz', 'col'))  12.1 us
    unnamed x105, local copies, waits for them, and re-layouts  11.5 us
    convert_element_type x1, other arithmetic, shards(): smoothed = smooth.astype(jnp.bfloat16)  11.2 us
    ppermute x4, waiting for transfers between devices, with_halo(): after = lax.ppermute(leading, axis, down)  9.77 us
    reduce_sum x3, other arithmetic, shards(): tile_terms.append(jnp.sum(shifted * grad_tile_vals, axis=(1, 2, 3)))  8.73 us
    ppermute x4, starting transfers between devices, with_halo(): before = lax.ppermute(last, axis, up)  7.05 us
  transfers between devices with their start and end apart: 9, of which 5 were waited for; matrix products, arithmetic and copies ran while one was open for 12% of the time, Pallas kernels for 0%

profile of v1, /device:TPU:0, one launch (start us, length us, event | category | flops | bytes accessed | tf_op | source)
XLA Modules:
  0.0 187.2 jit_solution(7558691039119144272)
XLA Ops:
  7.2 0.0 all-reduce.7.cloned.1.call-start
  7.2 1.1 copy.53
  8.4 3.1 %collective-permute-start = (bf16[32,32,2,128]{3,1,2,0:T(8,128)(2,1)S(1)}, bf16[32,32,2,128]{3,1,2,0:T(8,128)(2,1)S(1)}, u32[]{:S(2)}, u32[]{:S(2)}) collective-permute-start(bf16[32,32,2,128]{3,1,2,0:T(8,128)(2,1)S(1)} %copy.53), channel_id=1, source_target_pairs={{0,4},{4,8},{8,12},{12,0},{1,5},{5,9},{9,13},{13,1},{2,6},{6,10},{... | collective-permute-start | bytes 1572872 | tf_op jit(solution)/shard_map/ppermute | solution.py:14
  11.5 2.1 %collective-permute-start.1 = (bf16[32,32,2,128]{3,1,2,0:T(8,128)(2,1)S(1)}, bf16[32,32,2,128]{3,1,2,0:T(8,128)(2,1)S(1)}, u32[]{:S(2)}, u32[]{:S(2)}) collective-permute-start(bf16[32,32,2,128]{3,1,2,0:T(8,128)(2,1)S(1)} %copy.53), channel_id=1, source_target_pairs={{4,0},{8,4},{12,8},{0,12},{5,1},{9,5},{13,9},{1,13},{6,2},{10,6},{... | collective-permute-start | bytes 1572872 | tf_op jit(solution)/shard_map/ppermute | solution.py:15
  13.6 0.8 fusion.110
  14.4 0.1 fusion.117
  14.6 1.1 dynamic-slice_bitcast_fusion.8
  15.7 0.7 broadcast_multiply_fusion.4
  16.4 0.7 broadcast_multiply_fusion.2
  17.1 0.7 broadcast_multiply_fusion
  17.8 0.1 broadcast_multiply_fusion.6
  18.0 0.1 broadcast_multiply_fusion.16
  18.1 2.5 %slice_reduce_fusion.24 = (f32[32]{0:T(128)S(1)}, f32[32]{0:T(128)S(1)}, f32[32]{0:T(128)S(1)}, f32[32]{0:T(128)S(1)}, f32[32]{0:T(128)S(1)}, /*index=5*/f32[32]...) fusion(f32[32,25]{1,0:T(8,128)} %param.11), kind=kLoop, calls=%fused_computation.296 | loop fusion | bytes 4864 | tf_op jit(solution)/shard_map/slice | solution.py:117
  20.6 5.7 %collective-permute-done = bf16[32,32,2,128]{3,1,2,0:T(8,128)(2,1)S(1)} collective-permute-done((bf16[32,32,2,128]{3,1,2,0:T(8,128)(2,1)S(1)}, bf16[32,32,2,128]{3,1,2,0:T(8,128)(2,1)S(1)}, u32[]{:S(2)}, u32[]{:S(2)}) %collective-permute-start) | collective-permute-done | bytes 524320 | tf_op jit(solution)/shard_map/ppermute | solution.py:14
  26.3 1.4 constant_dynamic-update-slice_fusion.1
  27.7 8.4 %collective-permute-done.1 = bf16[32,32,2,128]{3,1,2,0:T(8,128)(2,1)S(1)} collective-permute-done((bf16[32,32,2,128]{3,1,2,0:T(8,128)(2,1)S(1)}, bf16[32,32,2,128]{3,1,2,0:T(8,128)(2,1)S(1)}, u32[]{:S(2)}, u32[]{:S(2)}) %collective-permute-start.1) | collective-permute-done | bytes 524320 | tf_op jit(solution)/shard_map/ppermute | solution.py:15
  36.1 0.8 copy-done.9
  36.9 0.1 constant_dynamic-update-slice_fusion
  37.0 1.9 %fusion.129 = (bf16[32,32,6,2]{3,1,2,0:T(8,128)(2,1)S(1)}, bf16[32,32,6,2]{3,1,2,0:T(8,128)(2,1)}) fusion(bf16[32,32,6,128]{3,1,2,0:T(8,128)(2,1)S(1)} %constant_dynamic-update-slice_fusion), kind=kLoop, calls=%fused_computation.345 | loop fusion | bytes 98304 | tf_op jit(solution)/shard_map/slice | solution.py:13
  38.9 3.1 %copy.56 = bf16[32,32,6,2]{1,0,3,2:T(8,128)(2,1)} copy(bf16[32,32,6,2]{3,1,2,0:T(8,128)(2,1)} %get-tuple-element.99) | data formatting | bytes 49152 | tf_op jit(solution)/shard_map/slice | solution.py:12
  42.0 1.5 collective-permute-start.2
  43.5 2.1 %copy.58 = bf16[32,32,6,2]{1,0,3,2:T(8,128)(2,1)} copy(bf16[32,32,6,2]{3,1,2,0:T(8,128)(2,1)S(1)} %get-tuple-element.98) | data formatting | bytes 49152 | tf_op jit(solution)/shard_map/slice | solution.py:13
  45.6 0.5 collective-permute-start.3
  46.2 0.8 slice_reduce_fusion.23
  47.0 2.2 %copy.57 = bf16[32,32,6,2]{3,1,2,0:T(8,128)(2,1)S(1)} copy(bf16[32,32,6,2]{1,0,3,2:T(8,128)(2,1)} %collective-permute-done.2) | data formatting | bytes 49152 | tf_op jit(solution)/shard_map/ppermute | solution.py:14
  49.2 1.4 collective-permute-done.3
  50.6 3.0 %copy.59 = bf16[32,32,6,2]{3,1,2,0:T(8,128)(2,1)} copy(bf16[32,32,6,2]{1,0,3,2:T(8,128)(2,1)} %collective-permute-done.3) | data formatting | bytes 49152 | tf_op jit(solution)/shard_map/ppermute | solution.py:15
  53.5 11.2 %fusion.90 = (bf16[32,32,2,128]{3,1,2,0:T(8,128)(2,1)S(1)}, bf16[32,32,2,128]{3,1,2,0:T(8,128)(2,1)}, bf16[32,32,2,128]{3,1,2,0:T(8,128)(2,1)}) fusion(bf16[32,32,2,128]{3,1,2,0:T(8,128)(2,1)} %copy-done.9, bf16[32,32,2,128]{3,1,2,0:T(8,128)(2,1)} %copy-done.5, bf16[32,32,2,128]{3,1,2,0:T(8,128)(2,1)} %copy-done.7, f32[32]{0:T(128)} %get-tuple-element.81, ...), kind=kLoop, calls=%fused_computation.211 | loop fusion | flops 37486592 | bytes 4770944 | tf_op jit(solution)/shard_map/convert_element_type | solution.py:65
  64.8 4.2 %all_to_all.36 = bf16[32,32,2,128]{3,1,2,0:T(8,128)(2,1)S(1)} all-to-all(bf16[32,32,2,128]{3,1,2,0:T(8,128)(2,1)S(1)} %get-tuple-element.91), channel_id=1, replica_groups=mesh['group'=2,'gx'=4,'gz'=2,'col'=2] {'col'}, dimensions={0} | all-to-all | bytes 1048576 | tf_op jit(solution)/shard_map/all_to_all | solution.py:71
  68.9 0.3 copy.63
  69.2 2.7 %fusion.88 = (f32[16,64,2,128]{3,0,2,1:T(8,128)S(1)}, f32[16,64,2,128]{3,0,2,1:T(8,128)}) fusion(f32[16,64]{0,1:T(8,128)S(1)} %get-tuple-element.141, f32[16,64]{0,1:T(8,128)S(1)} %get-tuple-element.143, f32[16,64]{0,1:T(8,128)S(1)} %get-tuple-element.137, f32[16,64]{0,1:T(8,128)S(1)} %get-tuple-element.145, bf16[16,64,2,128]{3,0,2,1:T(8,128)(2,1)S(1)} %bitcast.143, ...), kind=kLoop, calls=%fused_computation.209 | loop fusion | flops 7864320 | bytes 2658304 | tf_op jit(solution)/shard_map/mul | solution.py:77
  72.0 1.3 fusion.113
  73.4 18.9 %all-reduce.7.cloned.1.call-done = f32[4,64,2,128]{3,0,2,1:T(4,128)} async-done(((f32[4,64,2,128]{3,0,2,1:T(4,128)}), f32[4,64,2,128]{3,0,2,1:T(4,128)}) %all-reduce.7.cloned.1.call-update) | async-done | bytes 262160 | tf_op jit(solution)/shard_map/psum | solution.py:81
  92.3 4.8 %fusion.42 = (f32[16]{0:T(128)S(1)}, f32[16]{0:T(128)S(1)}, f32[16]{0:T(128)S(1)}, f32[16]{0:T(128)S(1)}, f32[16]{0:T(128)S(1)}, /*index=5*/f32[16]{0:T(128)S(1)...) fusion(f32[64]{0:T(128)} %copy-done.40, ...), kind=kOutput, calls=%fused_computation.162 | convolution fusion | flops 24838000 | bytes 2952516 | tf_op jit(solution)/shard_map/kc,kyxz->cyxz/dot_general | solution.py:86
  97.2 1.7 fusion.48
  99.0 4.3 %all_to_all.37 = bf16[16,64,2,128]{3,0,2,1:T(8,128)(2,1)S(1)} all-to-all(bf16[16,64,2,128]{3,0,2,1:T(8,128)(2,1)S(1)} %fusion.48), channel_id=1, replica_groups=mesh['group'=2,'gx'=4,'gz'=2,'col'=2] {'col'}, dimensions={1} | all-to-all | bytes 1048576 | tf_op jit(solution)/shard_map/all_to_all | solution.py:104
  103.2 0.2 copy.64
  103.5 3.9 %fusion.85 = (f32[32]{0:T(128)S(1)}, f32[32]{0:T(128)S(1)}, f32[32]{0:T(128)S(1)}, f32[32]{0:T(128)S(1)}, f32[32]{0:T(128)S(1)}, /*index=5*/f32[32]{0:T(128)S(1)}, f32[32]{0:T(128)S(1)}, f32[32]{0:T(128)S(1)}, f32[32]{0:T(128)S(1)}) fusion(bf16[2,16,32,2,128]{4,2,3,1,0:T(8,128)(2,1)S(1)} %copy.64, bf16[32,32,6,2]{3,1,2,0:T(8,128)(2,1)S(1)} %copy-done.3, ...), kind=kLoop, calls=%fused_computation.205 | loop fusion | flops 14417632 | bytes 2122880 | tf_op jit(solution)/shard_map/reduce_sum | solution.py:122
  107.5 3.8 %fusion.82 = (f32[32]{0:T(128)S(1)}, f32[32]{0:T(128)S(1)}, f32[32]{0:T(128)S(1)}, f32[32]{0:T(128)S(1)}, f32[32]{0:T(128)S(1)}, /*index=5*/f32[32]{0:T(128)S(1)}, f32[32]{0:T(128)S(1)}, f32[32]{0:T(128)S(1)}, f32[32]{0:T(128)S(1)}) fusion(bf16[2,16,32,2,128]{4,2,3,1,0:T(8,128)(2,1)S(1)} %copy.64, ...), kind=kLoop, calls=%fused_computation.202 | loop fusion | flops 14417632 | bytes 2122880 | tf_op jit(solution)/shard_map/reduce_sum | solution.py:122
  111.2 1.8 collective-permute-start.4
  113.0 2.1 %collective-permute-start.5 = (bf16[32,32,2,128]{3,1,2,0:T(8,128)(2,1)S(1)}, bf16[32,32,2,128]{3,1,2,0:T(8,128)(2,1)}, u32[]{:S(2)}, u32[]{:S(2)}) collective-permute-start(bf16[32,32,2,128]{3,1,2,0:T(8,128)(2,1)S(1)} %bitcast.137), channel_id=1, source_target_pairs={{4,0},{8,4},{12,8},{0,12},{5,1},{9,5},{13,9},{1,13},{6,2},{10,6},{... | collective-permute-start | bytes 1572872 | tf_op jit(solution)/shard_map/ppermute | solution.py:15
  115.1 1.1 fusion.84
  116.2 1.4 convolution_bitcast_fusion
  117.7 0.2 dynamic_update_slice.6
  117.9 0.1 dynamic_update_slice.7
  118.1 0.1 stack.133
  118.2 12.1 %all-reduce.3 = (f32[32,25]{0,1:T(8,128)S(1)}, f32[32,9]{0,1:T(8,128)S(1)}, f32[4,32]{1,0:T(4,128)S(1)}) all-reduce(f32[32,25]{0,1:T(8,128)S(1)} %stack.133, f32[32,9]{0,1:T(8,128)S(1)} %dynamic_update_slice.6, f32[4,32]{1,0:T(4,128)S(1)} %dynamic_update_slice.7), channel_id=1, replica_groups=mesh['group'=2,'gx'=4,'gz'=2,'col'=2] {'gz','col'}, use_global_device_ids=true, to_apply=%region_26.27 | all-reduce | flops 1216 | bytes 9728 | tf_op jit(solution)/shard_map/psum | solution.py:124
  130.2 19.1 %all-reduce.4 = (f32[32,25]{0,1:T(8,128)S(1)}, f32[32,9]{0,1:T(8,128)S(1)}, f32[4,32]{1,0:T(4,128)S(1)}) all-reduce(f32[32,25]{0,1:T(8,128)S(1)} %get-tuple-element.83, f32[32,9]{0,1:T(8,128)S(1)} %get-tuple-element.84, f32[4,32]{1,0:T(4,128)S(1)} %get-tuple-element.85), channel_id=1, replica_groups=mesh['group'=2,'gx'=4,'gz'=2,'col'=2] {'gx'}, use_global_device_ids=true, to_apply=%region_27.28 | all-reduce | flops 1216 | bytes 9728 | tf_op jit(solution)/shard_map/psum | solution.py:124
  149.3 0.6 broadcast_multiply_fusion.18
  149.9 0.8 copy-done.12
  150.7 1.4 pad_maximum_fusion.1
  152.1 2.4 %fusion.128 = (bf16[32,32,6,2]{3,1,2,0:T(8,128)(2,1)}, bf16[32,32,6,2]{3,1,2,0:T(8,128)(2,1)}) fusion(bf16[32,32,6,128]{3,1,2,0:T(8,128)(2,1)S(1)} %pad_maximum_fusion.1), kind=kLoop, calls=%fused_computation.344 | loop fusion | bytes 98304 | tf_op jit(solution)/shard_map/slice | solution.py:13
  154.5 2.6 %copy.75 = bf16[32,32,6,2]{1,0,3,2:T(8,128)(2,1)S(1)} copy(bf16[32,32,6,2]{3,1,2,0:T(8,128)(2,1)} %get-tuple-element.96) | data formatting | bytes 49152
  157.1 1.5 collective-permute-start.6
  158.6 2.5 %copy.76 = bf16[32,32,6,2]{1,0,3,2:T(8,128)(2,1)S(1)} copy(bf16[32,32,6,2]{3,1,2,0:T(8,128)(2,1)} %get-tuple-element.97) | data formatting | bytes 49152
  161.1 0.7 collective-permute-start.7
  161.8 0.6 broadcast_multiply_fusion.19
  162.4 0.7 copy.72
  163.1 1.4 copy.66
  164.5 1.3 collective-permute-done.7
  165.8 2.2 %copy.68 = bf16[32,32,6,2]{3,1,2,0:T(8,128)(2,1)} copy(bf16[32,32,6,2]{1,0,3,2:T(8,128)(2,1)S(1)} %collective-permute-done.7) | data formatting | bytes 49152 | tf_op jit(solution)/shard_map/ppermute | solution.py:14
  168.2 4.3 %pad_maximum_fusion = (bf16[32,32,6,130]{3,1,2,0:T(8,128)(2,1)S(1)}, bf16[32,32,6,130]{3,1,2,0:T(8,128)(2,1)S(1)}) fusion(bf16[32,32,6,2]{3,1,2,0:T(8,128)(2,1)S(1)} %copy.66, bf16[32,32,2,128]{3,1,2,0:T(8,128)(2,1)} %collective-permute-done.5, bf16[32,32,2,128]{3,1,2,0:T(8,128)(2,1)S(1)} %bitcast.139, bf16[32,32,2,128]{3,1,2,0:T(8,128)(2,1)S(1)} %copy-done.13, ...), kind=kLoop, calls=%fused_computation.72 | loop fusion | flops 12779520 | bytes 4816896 | tf_op jit(solution)/shard_map/concatenate | solution.py:16
  172.6 6.4 %fusion.89 = bf16[32,32,2,128]{3,1,2,0:T(8,128)(2,1)S(1)} fusion(bf16[32,32,2,128]{3,1,2,0:T(8,128)(2,1)S(1)} %copy-done.13, bf16[32,32,2,128]{3,1,2,0:T(8,128)(2,1)S(1)} %bitcast.140, bf16[32,32,2,128]{3,1,2,0:T(8,128)(2,1)} %collective-permute-done.5, bf16[32,32,6,130]{3,1,2,0:T(8,128)(2,1)S(1)} %get-tuple-element.95, ...), kind=kLoop, calls=%fused_computation.210 | loop fusion | flops 20185088 | bytes 12586112 | tf_op jit(solution)/shard_map/convert_element_type | solution.py:126
  179.0 1.3 copy.71
  (106 shorter events, 0.3 us)
Async XLA Ops:
  7.2 6.4 %copy-start = (f32[16,9]{1,0:T(8,128)S(1)}, f32[16,9]{1,0:T(8,128)}, u32[]{:S(2)}) copy-start(f32[16,9]{1,0:T(8,128)} %param.10) | copy-start | bytes 1732
  7.2 85.1 %all-reduce.7.cloned.1.call-start = ((), (), s32[]{:S(2)}) async-start(), calls=%async_computation.2 | async-start | bytes 524288 | tf_op jit(solution)/shard_map/psum | solution.py:81
  8.4 27.7 %copy-start.5 = (bf16[32,32,2,128]{3,1,2,0:T(8,128)(2,1)}, bf16[32,32,2,128]{3,1,2,0:T(8,128)(2,1)S(1)}, u32[]{:S(2)}) copy-start(bf16[32,32,2,128]{3,1,2,0:T(8,128)(2,1)S(1)} %copy.53) | copy-start | bytes 1572868
  8.4 17.9 %collective-permute-start = (bf16[32,32,2,128]{3,1,2,0:T(8,128)(2,1)S(1)}, bf16[32,32,2,128]{3,1,2,0:T(8,128)(2,1)S(1)}, u32[]{:S(2)}, u32[]{:S(2)}) collective-permute-start(bf16[32,32,2,128]{3,1,2,0:T(8,128)(2,1)S(1)} %copy.53), channel_id=1, source_target_pairs={{0,4},{4,8},{8,12},{12,0},{1,5},{5,9},{9,13},{13,1},{2,6},{6,10},{... | collective-permute-start | bytes 1572872 | tf_op jit(solution)/shard_map/ppermute | solution.py:14
  11.5 24.6 %collective-permute-start.1 = (bf16[32,32,2,128]{3,1,2,0:T(8,128)(2,1)S(1)}, bf16[32,32,2,128]{3,1,2,0:T(8,128)(2,1)S(1)}, u32[]{:S(2)}, u32[]{:S(2)}) collective-permute-start(bf16[32,32,2,128]{3,1,2,0:T(8,128)(2,1)S(1)} %copy.53), channel_id=1, source_target_pairs={{4,0},{8,4},{12,8},{0,12},{5,1},{9,5},{13,9},{1,13},{6,2},{10,6},{... | collective-permute-start | bytes 1572872 | tf_op jit(solution)/shard_map/ppermute | solution.py:15
  14.5 3.3 %copy-start.40 = (f32[64]{0:T(128)}, f32[64]{0:T(128)S(1)}, u32[]{:S(2)}) copy-start(f32[64]{0:T(128)S(1)} %get-tuple-element.108) | copy-start | bytes 772
  14.5 3.3 %copy-start.41 = (f32[64]{0:T(128)}, f32[64]{0:T(128)S(1)}, u32[]{:S(2)}) copy-start(f32[64]{0:T(128)S(1)} %get-tuple-element.109) | copy-start | bytes 772
  14.5 3.3 %copy-start.42 = (f32[64]{0:T(128)}, f32[64]{0:T(128)S(1)}, u32[]{:S(2)}) copy-start(f32[64]{0:T(128)S(1)} %get-tuple-element.110) | copy-start | bytes 772
  14.5 3.3 %copy-start.43 = (f32[64]{0:T(128)}, f32[64]{0:T(128)S(1)}, u32[]{:S(2)}) copy-start(f32[64]{0:T(128)S(1)} %get-tuple-element.111) | copy-start | bytes 772
  14.6 3.3 %copy-start.45 = (f32[64]{0:T(128)}, f32[64]{0:T(128)S(1)}, u32[]{:S(2)}) copy-start(f32[64]{0:T(128)S(1)} %get-tuple-element.113) | copy-start | bytes 772
  14.6 3.3 %copy-start.46 = (f32[64]{0:T(128)}, f32[64]{0:T(128)S(1)}, u32[]{:S(2)}) copy-start(f32[64]{0:T(128)S(1)} %get-tuple-element.114) | copy-start | bytes 772
  14.6 3.4 %copy-start.44 = (f32[64]{0:T(128)}, f32[64]{0:T(128)S(1)}, u32[]{:S(2)}) copy-start(f32[64]{0:T(128)S(1)} %get-tuple-element.112) | copy-start | bytes 772
  14.6 3.4 %copy-start.47 = (f32[64]{0:T(128)}, f32[64]{0:T(128)S(1)}, u32[]{:S(2)}) copy-start(f32[64]{0:T(128)S(1)} %get-tuple-element.115) | copy-start | bytes 772
  14.6 6.0 %copy-start.48 = (f32[64]{0:T(128)}, f32[64]{0:T(128)S(1)}, u32[]{:S(2)}) copy-start(f32[64]{0:T(128)S(1)} %get-tuple-element.116) | copy-start | bytes 772
  26.3 9.8 %copy-start.7 = (bf16[32,32,2,128]{3,1,2,0:T(8,128)(2,1)}, bf16[32,32,2,128]{3,1,2,0:T(8,128)(2,1)S(1)}, u32[]{:S(2)}) copy-start(bf16[32,32,2,128]{3,1,2,0:T(8,128)(2,1)S(1)} %collective-permute-done) | copy-start | bytes 1572868
  36.1 0.8 copy-start.9
  38.9 7.3 %copy-start.4 = (f32[32,25]{1,0:T(8,128)S(1)}, f32[32,25]{1,0:T(8,128)}, u32[]{:S(2)}) copy-start(f32[32,25]{1,0:T(8,128)} %param.11) | copy-start | bytes 9604
  42.0 5.0 %collective-permute-start.2 = (bf16[32,32,6,2]{1,0,3,2:T(8,128)(2,1)}, bf16[32,32,6,2]{1,0,3,2:T(8,128)(2,1)}, u32[]{:S(2)}, u32[]{:S(2)}) collective-permute-start(bf16[32,32,6,2]{1,0,3,2:T(8,128)(2,1)} %copy.56), channel_id=1, source_target_pairs={{0,2},{2,0},{1,3},{3,1},{4,6},{6,4},{5,7},{7,5},{8,10},{10,8},{9,1... | collective-permute-start | bytes 73736 | tf_op jit(solution)/shard_map/ppermute | solution.py:14
  45.6 4.9 %collective-permute-start.3 = (bf16[32,32,6,2]{1,0,3,2:T(8,128)(2,1)}, bf16[32,32,6,2]{1,0,3,2:T(8,128)(2,1)}, u32[]{:S(2)}, u32[]{:S(2)}) collective-permute-start(bf16[32,32,6,2]{1,0,3,2:T(8,128)(2,1)} %copy.58), channel_id=1, source_target_pairs={{2,0},{0,2},{3,1},{1,3},{6,4},{4,6},{7,5},{5,7},{10,8},{8,10},{11,... | collective-permute-start | bytes 73736 | tf_op jit(solution)/shard_map/ppermute | solution.py:15
  49.2 15.6 %copy-start.1 = (bf16[32,32,6,2]{3,1,2,0:T(8,128)(2,1)}, bf16[32,32,6,2]{3,1,2,0:T(8,128)(2,1)S(1)}, u32[]{:S(2)}) copy-start(bf16[32,32,6,2]{3,1,2,0:T(8,128)(2,1)S(1)} %copy.57) | copy-start | bytes 73732
  64.7 7.2 %copy-start.39 = (f32[4,32]{1,0:T(4,128)S(1)}, f32[4,32]{1,0:T(4,128)}, u32[]{:S(2)}) copy-start(f32[4,32]{1,0:T(4,128)} %param.13) | copy-start | bytes 1540
  92.3 4.9 %copy-start.17 = (f32[16,64]{0,1:T(8,128)S(1)}, f32[16,64]{0,1:T(8,128)}, u32[]{:S(2)}) copy-start(f32[16,64]{0,1:T(8,128)} %get-tuple-element.132) | copy-start | bytes 12292
  92.3 4.9 %copy-start.18 = (f32[16,64]{0,1:T(8,128)S(1)}, f32[16,64]{0,1:T(8,128)}, u32[]{:S(2)}) copy-start(f32[16,64]{0,1:T(8,128)} %get-tuple-element.148) | copy-start | bytes 12292
  92.3 4.9 %copy-start.19 = (f32[16,64]{0,1:T(8,128)S(1)}, f32[16,64]{0,1:T(8,128)}, u32[]{:S(2)}) copy-start(f32[16,64]{0,1:T(8,128)} %get-tuple-element.136) | copy-start | bytes 12292
  92.3 4.9 %copy-start.20 = (f32[16,64]{0,1:T(8,128)S(1)}, f32[16,64]{0,1:T(8,128)}, u32[]{:S(2)}) copy-start(f32[16,64]{0,1:T(8,128)} %get-tuple-element.146) | copy-start | bytes 12292
  92.3 4.9 %copy-start.21 = (f32[16,64]{0,1:T(8,128)S(1)}, f32[16,64]{0,1:T(8,128)}, u32[]{:S(2)}) copy-start(f32[16,64]{0,1:T(8,128)} %get-tuple-element.140) | copy-start | bytes 12292
  92.3 4.9 %copy-start.22 = (f32[16,64]{0,1:T(8,128)S(1)}, f32[16,64]{0,1:T(8,128)}, u32[]{:S(2)}) copy-start(f32[16,64]{0,1:T(8,128)} %get-tuple-element.144) | copy-start | bytes 12292
  97.1 6.3 %copy-start.3 = (bf16[32,32,6,2]{3,1,2,0:T(8,128)(2,1)S(1)}, bf16[32,32,6,2]{3,1,2,0:T(8,128)(2,1)}, u32[]{:S(2)}) copy-start(bf16[32,32,6,2]{3,1,2,0:T(8,128)(2,1)} %copy.59) | copy-start | bytes 73732
  98.9 8.5 %copy-start.2 = (bf16[32,32,6,2]{3,1,2,0:T(8,128)(2,1)S(1)}, bf16[32,32,6,2]{3,1,2,0:T(8,128)(2,1)}, u32[]{:S(2)}) copy-start(bf16[32,32,6,2]{3,1,2,0:T(8,128)(2,1)} %copy-done.1) | copy-start | bytes 73732
  103.5 11.6 %copy-start.6 = (bf16[32,32,2,128]{3,1,2,0:T(8,128)(2,1)S(1)}, bf16[32,32,2,128]{3,1,2,0:T(8,128)(2,1)}, u32[]{:S(2)}) copy-start(bf16[32,32,2,128]{3,1,2,0:T(8,128)(2,1)} %copy-done.5) | copy-start | bytes 1572868
  103.5 11.6 %copy-start.8 = (bf16[32,32,2,128]{3,1,2,0:T(8,128)(2,1)S(1)}, bf16[32,32,2,128]{3,1,2,0:T(8,128)(2,1)}, u32[]{:S(2)}) copy-start(bf16[32,32,2,128]{3,1,2,0:T(8,128)(2,1)} %copy-done.7) | copy-start | bytes 1572868
  103.5 11.6 %copy-start.10 = (bf16[32,32,2,128]{3,1,2,0:T(8,128)(2,1)S(1)}, bf16[32,32,2,128]{3,1,2,0:T(8,128)(2,1)}, u32[]{:S(2)}) copy-start(bf16[32,32,2,128]{3,1,2,0:T(8,128)(2,1)} %copy-done.9) | copy-start | bytes 1572868
  103.5 11.6 %copy-start.11 = (bf16[32,32,2,128]{3,2,1,0:T(2,128)(2,1)S(1)}, bf16[32,32,2,128]{3,2,1,0:T(2,128)(2,1)}, u32[]{:S(2)}) copy-start(bf16[32,32,2,128]{3,2,1,0:T(2,128)(2,1)} %param.7) | copy-start | bytes 1572868
  103.5 11.6 %copy-start.14 = (bf16[32,32,2,128]{3,1,2,0:T(8,128)(2,1)S(1)}, bf16[32,32,2,128]{3,1,2,0:T(8,128)(2,1)}, u32[]{:S(2)}) copy-start(bf16[32,32,2,128]{3,1,2,0:T(8,128)(2,1)} %get-tuple-element.92) | copy-start | bytes 1572868
  103.5 11.6 %copy-start.15 = (bf16[32,32,2,128]{3,1,2,0:T(8,128)(2,1)S(1)}, bf16[32,32,2,128]{3,1,2,0:T(8,128)(2,1)}, u32[]{:S(2)}) copy-start(bf16[32,32,2,128]{3,1,2,0:T(8,128)(2,1)} %get-tuple-element.93) | copy-start | bytes 1572868
  107.4 8.8 %copy-start.16 = (f32[4,64,2,128]{3,0,2,1:T(4,128)S(1)}, f32[4,64,2,128]{3,0,2,1:T(4,128)}, u32[]{:S(2)}) copy-start(f32[4,64,2,128]{3,0,2,1:T(4,128)} %all-reduce.7.cloned.1.call-done) | copy-start | bytes 786436
  107.4 8.8 %copy-start.23 = (s32[64,2,128]{2,1,0:T(2,128)S(1)}, s32[64,2,128]{2,1,0:T(2,128)}, u32[]{:S(2)}) copy-start(s32[64,2,128]{2,1,0:T(2,128)} %param.8) | copy-start | bytes 196612
  111.2 38.7 %collective-permute-start.4 = (bf16[32,32,2,128]{3,1,2,0:T(8,128)(2,1)S(1)}, bf16[32,32,2,128]{3,1,2,0:T(8,128)(2,1)S(1)}, u32[]{:S(2)}, u32[]{:S(2)}) collective-permute-start(bf16[32,32,2,128]{3,1,2,0:T(8,128)(2,1)S(1)} %bitcast.136), channel_id=1, source_target_pairs={{0,4},{4,8},{8,12},{12,0},{1,5},{5,9},{9,13},{13,1},{2,6},{6,10},{... | collective-permute-start | bytes 1572872 | tf_op jit(solution)/shard_map/ppermute | solution.py:14
  113.0 37.7 %collective-permute-start.5 = (bf16[32,32,2,128]{3,1,2,0:T(8,128)(2,1)S(1)}, bf16[32,32,2,128]{3,1,2,0:T(8,128)(2,1)}, u32[]{:S(2)}, u32[]{:S(2)}) collective-permute-start(bf16[32,32,2,128]{3,1,2,0:T(8,128)(2,1)S(1)} %bitcast.137), channel_id=1, source_target_pairs={{4,0},{8,4},{12,8},{0,12},{5,1},{9,5},{13,9},{1,13},{6,2},{10,6},{... | collective-permute-start | bytes 1572872 | tf_op jit(solution)/shard_map/ppermute | solution.py:15
  149.9 0.8 copy-start.12
  154.5 13.5 %copy-start.13 = (bf16[32,32,2,128]{3,1,2,0:T(8,128)(2,1)S(1)}, bf16[32,32,2,128]{3,1,2,0:T(8,128)(2,1)}, u32[]{:S(2)}) copy-start(bf16[32,32,2,128]{3,1,2,0:T(8,128)(2,1)} %copy-done.12) | copy-start | bytes 1572868
  157.1 6.0 %collective-permute-start.6 = (bf16[32,32,6,2]{1,0,3,2:T(8,128)(2,1)S(1)}, bf16[32,32,6,2]{1,0,3,2:T(8,128)(2,1)S(1)}, u32[]{:S(2)}, u32[]{:S(2)}) collective-permute-start(bf16[32,32,6,2]{1,0,3,2:T(8,128)(2,1)S(1)} %copy.75), channel_id=1, source_target_pairs={{2,0},{0,2},{3,1},{1,3},{6,4},{4,6},{7,5},{5,7},{10,8},{8,10},{11,... | collective-permute-start | bytes 73736 | tf_op jit(solution)/shard_map/ppermute | solution.py:15
  161.1 4.7 %collective-permute-start.7 = (bf16[32,32,6,2]{1,0,3,2:T(8,128)(2,1)S(1)}, bf16[32,32,6,2]{1,0,3,2:T(8,128)(2,1)S(1)}, u32[]{:S(2)}, u32[]{:S(2)}) collective-permute-start(bf16[32,32,6,2]{1,0,3,2:T(8,128)(2,1)S(1)} %copy.76), channel_id=1, source_target_pairs={{0,2},{2,0},{1,3},{3,1},{4,6},{6,4},{5,7},{7,5},{8,10},{10,8},{9,1... | collective-permute-start | bytes 73736 | tf_op jit(solution)/shard_map/ppermute | solution.py:14
  168.0 4.4 %copy-start.24 = (f32[32]{0:T(128)S(1)}, f32[32]{0:T(128)}, u32[]{:S(2)}) copy-start(f32[32]{0:T(128)} %get-tuple-element.64) | copy-start | bytes 388
  168.0 4.4 %copy-start.25 = (f32[32]{0:T(128)S(1)}, f32[32]{0:T(128)}, u32[]{:S(2)}) copy-start(f32[32]{0:T(128)} %get-tuple-element.65) | copy-start | bytes 388
  168.0 4.4 %copy-start.26 = (f32[32]{0:T(128)S(1)}, f32[32]{0:T(128)}, u32[]{:S(2)}) copy-start(f32[32]{0:T(128)} %get-tuple-element.66) | copy-start | bytes 388
  168.0 4.4 %copy-start.27 = (f32[32]{0:T(128)S(1)}, f32[32]{0:T(128)}, u32[]{:S(2)}) copy-start(f32[32]{0:T(128)} %get-tuple-element.67) | copy-start | bytes 388
  168.0 4.4 %copy-start.28 = (f32[32]{0:T(128)S(1)}, f32[32]{0:T(128)}, u32[]{:S(2)}) copy-start(f32[32]{0:T(128)} %get-tuple-element.68) | copy-start | bytes 388
  168.1 4.4 %copy-start.29 = (f32[32]{0:T(128)S(1)}, f32[32]{0:T(128)}, u32[]{:S(2)}) copy-start(f32[32]{0:T(128)} %get-tuple-element.69) | copy-start | bytes 388
  168.1 4.4 %copy-start.30 = (f32[32]{0:T(128)S(1)}, f32[32]{0:T(128)}, u32[]{:S(2)}) copy-start(f32[32]{0:T(128)} %get-tuple-element.70) | copy-start | bytes 388
  168.1 4.4 %copy-start.31 = (f32[32]{0:T(128)S(1)}, f32[32]{0:T(128)}, u32[]{:S(2)}) copy-start(f32[32]{0:T(128)} %get-tuple-element.71) | copy-start | bytes 388
  168.1 4.4 %copy-start.32 = (f32[32]{0:T(128)S(1)}, f32[32]{0:T(128)}, u32[]{:S(2)}) copy-start(f32[32]{0:T(128)} %get-tuple-element.72) | copy-start | bytes 388
  168.1 4.4 %copy-start.33 = (f32[32]{0:T(128)S(1)}, f32[32]{0:T(128)}, u32[]{:S(2)}) copy-start(f32[32]{0:T(128)} %get-tuple-element.73) | copy-start | bytes 388
  168.1 4.4 %copy-start.34 = (f32[32]{0:T(128)S(1)}, f32[32]{0:T(128)}, u32[]{:S(2)}) copy-start(f32[32]{0:T(128)} %get-tuple-element.74) | copy-start | bytes 388
  168.1 4.4 %copy-start.35 = (f32[32]{0:T(128)S(1)}, f32[32]{0:T(128)}, u32[]{:S(2)}) copy-start(f32[32]{0:T(128)} %get-tuple-element.75) | copy-start | bytes 388
  168.1 4.4 %copy-start.36 = (f32[32]{0:T(128)S(1)}, f32[32]{0:T(128)}, u32[]{:S(2)}) copy-start(f32[32]{0:T(128)} %get-tuple-element.76) | copy-start | bytes 388
  168.1 4.4 %copy-start.37 = (f32[32]{0:T(128)S(1)}, f32[32]{0:T(128)}, u32[]{:S(2)}) copy-start(f32[32]{0:T(128)} %get-tuple-element.81) | copy-start | bytes 388
  168.1 4.4 %copy-start.38 = (f32[32]{0:T(128)S(1)}, f32[32]{0:T(128)}, u32[]{:S(2)}) copy-start(f32[32]{0:T(128)} %get-tuple-element.82) | copy-start | bytes 388
Sparse Core Ops, SparseCore 0:
  73.5 18.7 all-reduce.6
